TPU v7x, 768 devices: a whole 4x8x12 slice. The times are simulated.
768 devices in a mesh: blk: 64 (over z_lo, y, core), grp: 12 (over z_hi, x).
Axes of the slice: x: 4, y: 8, z: 12 (z_hi: 3, z_lo: 4; z = z_hi * 4 + z_lo), core: 2. Of those that a mesh axis runs over, the one named last changes fastest.
Arguments:
- user_embed: float32 [98304, 256], P(('blk', 'grp')), may hold values from -6 to 6
- item_embed: float32 [12, 4096, 256], P('grp', 'blk'), may hold values from -6 to 6
- user_degree: int32 [98304], P(('blk', 'grp')), may hold values from 1 to 99
- item_degree: int32 [12, 4096], P('grp', 'blk'), may hold values from 1 to 99
- tile_values: bfloat16 [2048, 24, 128, 128], P('blk', 'grp'), may hold values from 0.049804688 to 1
- tile_rows: int32 [2048, 24], P('blk', 'grp'), may hold values from 0 to 12, as said below
Outputs:
- user_out: float32 [98304, 256], P(('blk', 'grp'))
- item_out: float32 [12, 4096, 256], P('grp', 'blk')
Inputs may be any that keep to these rules, and one draw needn't show every extreme that they name: `tile_rows`: within one column block of one device the live slots name different row blocks, the first slot is always live, and a slot that holds 12 is empty.
All inputs are finite; a program needn't handle non-finite values.
Results may differ from a plain program's by a relative error of at most 0.0027.
Values may be sent and summed in bfloat16 or wider, within the bound.
A program may use at most 64 MiB of HBM per device.

v0:
```python
import jax
import jax.numpy as jnp
from jax import lax
from jax.sharding import PartitionSpec as P


def on_device(user_embed, item_embed, user_degree, item_degree, tile_values, tile_rows):
    tile_size = tile_values.shape[2]
    blocks = tile_values.shape[0]
    width = user_embed.shape[1]
    groups = lax.axis_size("grp")
    own_items = item_embed[0]
    half_rows = own_items.shape[0]
    scaled_items = (own_items * lax.rsqrt(item_degree[0].astype(jnp.float32))[:, None]).astype(
        jnp.bfloat16
    )
    scaled_users = (user_embed * lax.rsqrt(user_degree.astype(jnp.float32))[:, None]).astype(
        jnp.bfloat16
    )
    piece = lax.all_gather(scaled_items, "blk", axis=0, tiled=True)
    count = piece.shape[0]
    cover = min(count // tile_size + 1, blocks)
    tiles = tile_values
    products = jnp.einsum(
        "cstj,cjd->cstd",
        tiles,
        piece.reshape(cover, tile_size, width),
        preferred_element_type=jnp.float32,
    )
    summed = jnp.zeros((groups + 1, tile_size, width), jnp.float32)
    summed = summed.at[tile_rows.reshape(-1)].add(products.reshape(-1, tile_size, width))
    partial_users = summed[:groups].reshape(-1, width)
    user_sums = lax.psum_scatter(partial_users, "grp", scatter_dimension=0, tiled=True)
    row_vectors = lax.all_gather(scaled_users, "grp", axis=0, tiled=True)
    padded_users = jnp.concatenate(
        [
            row_vectors.reshape(groups, tile_size, width),
            jnp.zeros((1, tile_size, width), jnp.bfloat16),
        ],
        0,
    )
    cover = min(half_rows * lax.axis_size("blk") // tile_size + 1, blocks)
    tiles = tile_values
    selected = jnp.take(padded_users, tile_rows, axis=0)
    partial_items = jnp.einsum(
        "cstj,cstd->cjd", tiles, selected, preferred_element_type=jnp.float32
    )
    partial_items = partial_items.reshape(cover * tile_size, width)
    item_sums = lax.psum_scatter(partial_items, "blk", scatter_dimension=0, tiled=True)
    user_out = 0.5 * (user_embed + lax.rsqrt(user_degree.astype(jnp.float32))[:, None] * user_sums)
    item_new = 0.5 * (
        own_items + lax.rsqrt(item_degree[0].astype(jnp.float32))[:, None] * item_sums
    )
    return (user_out, item_new[None])


def solution(mesh):
    return jax.shard_map(
        on_device,
        mesh=mesh,
        in_specs=(
            P(("blk", "grp"), None),
            P("grp", "blk", None),
            P(("blk", "grp")),
            P("grp", "blk"),
            P("blk", "grp", None, None),
            P("blk", "grp"),
        ),
        out_specs=(P(("blk", "grp"), None), P("grp", "blk", None)),
        check_vma=False,
    )
```

profile of v0, /device:TPU:1, one launch (start us, length us, event | category | flops | bytes accessed | tf_op | source)
XLA Modules:
  0.0 702.1 jit_solution(1105951618432663460)
XLA Ops:
  7.2 0.0 all-gather.2.cloned.1.call-start
  7.2 0.8 rsqrt_bitcast_fusion
  8.0 1.5 fusion.4
  9.6 0.0 reduce-scatter.3.cloned.1.call-start
  9.6 0.8 copy.12
  10.4 0.1 reshape.64
  10.5 129.8 %all-gather.2.cloned.1.call-done = bf16[4096,256]{1,0:T(8,128)(2,1)} async-done(((bf16[64,256]{1,0:T(8,128)(2,1)}), bf16[4096,256]{1,0:T(8,128)(2,1)}) %all-gather.2.cloned.1.call-update) | async-done | bytes 2097168 | tf_op jit(solution)/shard_map/all_gather | solution.py:20
  140.3 6.1 fusion.9
  146.4 9.0 %copy.14 = f32[64,128,256]{2,1,0:T(8,128)} copy(f32[64,128,256]{1,2,0:T(8,128)} %bitcast.35) | data formatting | bytes 16777216 | tf_op jit(solution)/shard_map/reshape | solution.py:31
  155.4 1.4 broadcast_in_dim.24
  156.8 18.5 %scatter_fusion = f32[13,128,256]{2,1,0:T(8,128)} fusion(f32[13,128,256]{2,1,0:T(8,128)} %broadcast_in_dim.24, s32[64]{0:T(128)S(1)} %fusion.7, f32[64,128,256]{2,1,0:T(8,128)} %copy.14), kind=kCustom, calls=%fused_computation.1 | custom fusion | flops 2097152 | bytes 25166080 | tf_op jit(solution)/shard_map/scatter-add | solution.py:31
  175.3 2.7 slice.6
  178.0 0.0 reduce-scatter.5.cloned.1.call-start
  178.1 0.1 copy.16
  178.2 0.1 reshape.72
  178.3 0.1 copy.15
  178.5 168.7 %reduce-scatter.3.cloned.1.call-done = f32[128,256]{1,0:T(8,128)} async-done(((f32[1536,256]{1,0:T(8,128)}), f32[128,256]{1,0:T(8,128)}) %reduce-scatter.3.cloned.1.call-update) | async-done | bytes 131088 | tf_op jit(solution)/shard_map/reduce_scatter | solution.py:33
  347.2 1.6 multiply_convert_fusion
  348.9 47.6 %all_gather.7 = bf16[1536,256]{1,0:T(8,128)(2,1)S(1)} all-gather(bf16[128,256]{1,0:T(8,128)(2,1)S(1)} %get-tuple-element.2), channel_id=1, replica_groups=mesh['blk'=64,'grp'=12] {'grp'}, dimensions={0}, use_global_device_ids=true | all-gather | bytes 851968 | tf_op jit(solution)/shard_map/all_gather | solution.py:34
  396.5 0.1 concatenate.3
  396.6 2.8 gather_fusion
  399.4 5.1 fusion
  404.5 289.6 %reduce-scatter.5.cloned.1.call-done = f32[64,256]{1,0:T(8,128)} async-done(((f32[4096,256]{1,0:T(8,128)}), f32[64,256]{1,0:T(8,128)}) %reduce-scatter.5.cloned.1.call-update) | async-done | bytes 65552 | tf_op jit(solution)/shard_map/reduce_scatter | solution.py:49
  694.1 1.5 fusion.6
  (18 shorter events, 0.1 us)
Async XLA Ops:
  7.2 133.1 %copy-start = (bf16[32,2,128,128]{3,2,1,0:T(8,128)(2,1)S(1)}, bf16[32,2,128,128]{3,2,1,0:T(8,128)(2,1)}, u32[]{:S(2)}) copy-start(bf16[32,2,128,128]{3,2,1,0:T(8,128)(2,1)} %param.10) | copy-start | bytes 6291460
  7.2 133.1 %all-gather.2.cloned.1.call-start = ((), (), s32[]{:S(2)}) async-start(), calls=%async_computation.2 | async-start | bytes 2129920 | tf_op jit(solution)/shard_map/all_gather | solution.py:20
  9.6 337.6 %reduce-scatter.3.cloned.1.call-start = ((), (), s32[]{:S(2)}) async-start(), calls=%async_computation.3 | async-start | bytes 1703936 | tf_op jit(solution)/shard_map/reduce_scatter | solution.py:33
  175.3 2.8 copy-start.3
  175.3 3.1 copy-start.4
  175.3 171.9 %copy-start.2 = (f32[128,256]{1,0:T(8,128)S(1)}, f32[128,256]{1,0:T(8,128)}, u32[]{:S(2)}) copy-start(f32[128,256]{1,0:T(8,128)} %param.6) | copy-start | bytes 393220
  178.0 516.0 %reduce-scatter.5.cloned.1.call-start = ((), (), s32[]{:S(2)}) async-start(), calls=%async_computation.4 | async-start | bytes 4259840 | tf_op jit(solution)/shard_map/reduce_scatter | solution.py:49
  404.4 289.6 %copy-start.1 = (f32[1,64,256]{2,1,0:T(8,128)S(1)}, f32[1,64,256]{2,1,0:T(8,128)}, u32[]{:S(2)}) copy-start(f32[1,64,256]{2,1,0:T(8,128)} %param.7) | copy-start | bytes 196612
Sparse Core Ops, SparseCore 0:
  11.0 129.2 all-gather.1
  178.2 168.9 reduce-scatter.2
  404.6 289.4 reduce-scatter.4
where the time goes:
time: 706 us; the launch traced here: 702 us
  waiting for transfers between devices  588 us (83%)
  blocking collectives  47.6 us (7%)
  other arithmetic  24.1 us (3%)
  local copies, waits for them, and re-layouts  17.2 us (2%)
  between operations  13.8 us (2%)
  matrix products  11.2 us (2%)
    reduce_scatter x1, waiting for transfers between devices, on_device(): lax.psum_scatter(partial_items, 'blk', scatter_dimension=0, tiled=True)  290 us
    reduce_scatter x1, waiting for transfers between devices, on_device(): lax.psum_scatter(partial_users, 'grp', scatter_dimension=0, tiled=True)  169 us
    all_gather x1, waiting for transfers between devices, on_device(): piece = lax.all_gather(scaled_items, 'blk', axis=0, tiled=True)  130 us
    all_gather x1, blocking collectives, on_device(): row_vectors = lax.all_gather(scaled_users, 'grp', axis=0, tiled=True)  47.6 us
    scatter-add x1, other arithmetic, on_device(): summed.at[tile_rows.reshape(-1)].add(products.reshape(-1, tile_size, width))  18.5 us
  transfers between devices with their start and end apart: 3, of which 3 were waited for; matrix products, arithmetic and copies ran while one was open for 0% of the time, Pallas kernels for 0%

commit v1 on v0

v1 whole, which is shorter than its diff:
```python
import jax
import jax.numpy as jnp
from jax import lax
from jax.experimental import pallas as pl
from jax.experimental.pallas import tpu as pltpu
from jax.sharding import PartitionSpec as P

NZ, NY, NC = 4, 8, 2
NH, NX = 3, 4
TILE = 128
HALF = 64
D = 256
COLS = NZ * NY
SLOTS = 2
NT = COLS * SLOTS
ROWS = NH * NX
F32, BF16 = jnp.float32, jnp.bfloat16
MESH = pl.DeviceIdType.MESH
GROUPS = (4, 3, -3, 2, -2, 1, -1, 0)


def valid_gather(d, s, p):
    return s <= 2 or (s == 3 and p == d)


def column(row):
    n = row.shape[1]
    a = lax.broadcasted_iota(jnp.int32, (n, n), 0)
    b = lax.broadcasted_iota(jnp.int32, (n, n), 1)
    return jnp.sum(jnp.where(a == b, jnp.broadcast_to(row, (n, n)), 0.0), axis=1, keepdims=True)


def kernel(
    ue, ie, ud, ideg, tv, rows, uo, io,
    X, U, T, TT, S, PS, R, SB, RB, ZS, ZR, VS0, VR0, VS1, VR1, US, UR, keys, plan, order,
    tsem, osem, send, xz, xy, xs, uz, ux, uh, ps, ry, rz, v0, v1, vz,
):
    b = lax.axis_index("blk")
    g = lax.axis_index("grp")
    core = b % 2
    y = (b // 2) % NY
    zl = b // (2 * NY)
    x = g % NX
    zh = g // NX
    other = 1 - core

    def blk(z_, y_, c_):
        return {"blk": (z_ * NY + y_) * NC + c_}

    def grp(h_, x_):
        return {"grp": h_ * NX + x_}

    sib = blk(zl, y, other)
    ydev = (blk(zl, (y + 1) % NY, core), blk(zl, (y + NY - 1) % NY, core))
    zrel = (zl, zl + 1 - 2 * (zl % 2), (zl + 2) % NZ, NZ - 1 - zl)
    zdev = tuple(blk(z_, y, core) for z_ in zrel)
    xdev = (grp(zh, (x + 1) % NX), grp(zh, (x + NX - 1) % NX))
    hrel = (zh, (zh + NH - 1) % NH, (zh + 1) % NH)
    hdev = (None, grp(hrel[1], x), grp(hrel[2], x))
    pb0 = (zl // 2) * 2
    pb = (pb0, 2 - pb0)

    bar = pltpu.get_barrier_semaphore()
    peers = (sib,) + ydev + zdev[1:] + xdev + hdev[1:]
    for dev in peers:
        pl.semaphore_signal(bar, inc=1, device_id=dev, device_id_type=MESH)

    tcopy = pltpu.make_async_copy(tv, T, tsem)
    tcopy.start()

    sends = []

    def put(src, dst, rsem, dev):
        c = pltpu.make_async_remote_copy(
            src_ref=src, dst_ref=dst, send_sem=send.at[len(sends)], recv_sem=rsem,
            device_id=dev, device_id_type=MESH,
        )
        c.start()
        sends.append(c)

    def got(dst, rsem, dev):
        pltpu.make_async_remote_copy(
            src_ref=dst, dst_ref=dst, send_sem=send.at[0], recv_sem=rsem,
            device_id=dev, device_id_type=MESH,
        ).wait_recv()

    iscale = column(lax.rsqrt(ideg[...].astype(F32)))
    uscale = column(lax.rsqrt(ud[...].astype(F32)))
    X[y * NZ + zl, core] = (ie[...] * iscale).astype(BF16)
    U[g] = (ue[...] * uscale).astype(BF16)
    U[ROWS] = jnp.zeros((TILE, D), BF16)

    pl.semaphore_wait(bar, len(peers))

    own = X.at[y * NZ + zl, core]
    for k in (1, 3, 2):
        put(own, own, xz.at[k - 1], zdev[k])
    for j in (1, 2):
        put(U.at[g], U.at[g], uz.at[2 - j], hdev[j])
    for d in (0, 1):
        put(U.at[g], U.at[g], ux.at[d, 0], xdev[d])

    def xreg(yy, p, c):
        return X.at[pl.ds(yy * NZ + pb[p], 2), c]

    def yfrom(d, s):
        return (y + NY - 1 - s) % NY if d == 0 else (y + 1 + s) % NY

    for i in range(NT):
        keys[i : i + 1, :] = jnp.full((1, 128), rows[i // SLOTS, i % SLOTS], jnp.int32)
    kc = keys[...]
    sub = lax.broadcasted_iota(jnp.int32, (NT, 128), 0)
    lane = lax.broadcasted_iota(jnp.int32, (NT, 128), 1)
    uc = kc * NT + sub
    ur = jnp.sum(jnp.where(sub == lane, uc, 0), axis=0, keepdims=True)
    ur = jnp.where(lax.broadcasted_iota(jnp.int32, (1, 128), 1) < NT, ur, 1 << 20)
    rank = jnp.sum(jnp.where(ur < uc, 1, 0), axis=1, keepdims=True)
    hit = rank == lane
    plan[...] = jnp.zeros((8, 128), jnp.int32)
    plan[0:1, :] = jnp.sum(jnp.where(hit, sub, 0), axis=0, keepdims=True)
    plan[1:2, :] = jnp.sum(jnp.where(hit, kc, 0), axis=0, keepdims=True)
    upto = jnp.sum(jnp.where(kc <= lane, 1, 0), axis=0, keepdims=True)
    count = jnp.sum(jnp.where(kc == lane, 1, 0), axis=0, keepdims=True)
    plan[2:3, :] = jnp.where(count > 0, upto, 0)
    ocopy = pltpu.make_async_copy(plan, order, osem)
    ocopy.start()

    def xfirst(p):
        for d in (0, 1):
            put(xreg(y, p, core), xreg(y, p, core), xy.at[d, 0, p], ydev[d])

    def zgot(k):
        r = X.at[y * NZ + zrel[k], core]
        got(r, xz.at[k - 1], zdev[k])

    zgot(1)
    xfirst(0)
    zgot(3)
    zgot(2)
    xfirst(1)
    r = X.at[pl.ds(y * NZ, NZ), core]
    put(r, r, xs.at[0, 4, 0], sib)

    tcopy.wait()

    def flip(c, _):
        TT[c, :, 0:TILE] = T[2 * c].T
        TT[c, :, TILE:] = T[2 * c + 1].T
        return 0

    lax.fori_loop(0, COLS, flip, 0)

    def uslot(j, x_):
        return hrel[j] * NX + x_

    xnb = ((x + NX - 1) % NX, (x + 1) % NX)

    def users_pass(j):
        for d in (0, 1):
            s = uslot(j, xnb[d])
            got(U.at[s], ux.at[d, j], xdev[1 - d])
            h = U.at[s, pl.ds(d * HALF, HALF)]
            put(h, h, uh.at[d, j], xdev[d])

    def users_far(j):
        s = uslot(j, (x + 2) % NX)
        for d in (0, 1):
            got(U.at[s, pl.ds(d * HALF, HALF)], uh.at[d, j], xdev[1 - d])

    def items_pass(s):
        for p in (0, 1):
            for d in (0, 1):
                if not valid_gather(d, s, p):
                    continue
                yy = yfrom(d, s)
                r = xreg(yy, p, core)
                got(r, xy.at[d, s, p], ydev[1 - d])
                if valid_gather(d, s + 1, p):
                    put(r, r, xy.at[d, s + 1, p], ydev[d])
                put(r, r, xs.at[d, s, p], sib)

    users_pass(0)
    items_pass(0)
    for j in (1, 2):
        s = uslot(j, x)
        got(U.at[s], uz.at[j - 1], hdev[j])
        for d in (0, 1):
            put(U.at[s], U.at[s], ux.at[d, j], xdev[d])
    items_pass(1)
    users_pass(1)
    users_pass(2)
    items_pass(2)
    for j in (0, 1, 2):
        users_far(j)

    for i, off in enumerate(GROUPS):
        yd = (y + NY + off) % NY

        def one(z_, _, yd=yd):
            c = z_ * NY + yd
            lhs = TT[c]
            rhs = jnp.concatenate([U[rows[c, 0]], U[rows[c, 1]]], axis=0)
            out = jnp.dot(lhs, rhs, preferred_element_type=F32)
            PS[yd * NZ + z_] = out.reshape(NC, HALF, D)
            return 0

        lax.fori_loop(0, NZ, one, 0)
        put(PS.at[pl.ds(yd * NZ, NZ), other], R.at[pl.ds(yd * NZ, NZ)], ps.at[i], sib)

    items_pass(3)

    def pgot(i):
        yd = (y + NY + GROUPS[i]) % NY
        got(R.at[pl.ds(yd * NZ, NZ)], ps.at[i], sib)

    def sum_step(d, s, p):
        yd = (y + 4 - s) % NY if d == 0 else (y + NY - 4 + s) % NY
        q = pl.ds(yd * NZ + pb[p], 2)
        val = PS[q, core] + R[q]
        if not (s == 0 or (s == 1 and p != d)):
            got(RB.at[d, s - 1, p], ry.at[d, s - 1, p], ydev[1 - d])
            val = val + RB[d, s - 1, p].astype(F32)
        SB[d, s, p] = val.astype(BF16)
        put(SB.at[d, s, p], RB.at[d, s, p], ry.at[d, s, p], ydev[d])

    pgot(0)
    sum_step(0, 0, 0)
    sum_step(1, 0, 1)
    pgot(1)
    pgot(2)
    sum_step(0, 1, 1)
    sum_step(1, 1, 0)

    r = X.at[pl.ds(y * NZ, NZ), other]
    got(r, xs.at[0, 4, 0], sib)
    for s in range(4):
        for p in (0, 1):
            for d in (0, 1):
                if valid_gather(d, s, p):
                    got(xreg(yfrom(d, s), p, other), xs.at[d, s, p], sib)
    ocopy.wait()

    S[0] = jnp.zeros((TILE, D), F32)

    def forward(k, _):
        o = order[0, k]
        c = o // SLOTS
        keep = jnp.where(order[1, k] == order[1, jnp.maximum(k - 1, 0)], 1.0, 0.0)
        xb = X[(c % NY) * NZ + c // NY].reshape(TILE, D)
        S[k + 1] = S[k] * keep + jnp.dot(T[o], xb, preferred_element_type=F32)
        return 0

    lax.fori_loop(0, NT // 2, forward, 0)
    sum_step(0, 1, 0)
    sum_step(1, 1, 1)
    lax.fori_loop(NT // 2, NT, forward, 0)

    def user_sum(h_, x_):
        return S[order[2, h_ * NX + x_]]

    for h in range(NH):
        v = user_sum(h, (x + 2) % NX).astype(BF16)
        for d in (0, 1):
            VS0[d, h] = v[d * HALF : (d + 1) * HALF]
    for d in (0, 1):
        put(VS0.at[d], VR0.at[d], v0.at[d], xdev[d])

    pgot(3)
    pgot(4)
    for p in (0, 1):
        for d in (0, 1):
            sum_step(d, 2, p)

    for d in (0, 1):
        got(VR0.at[d], v0.at[d], xdev[1 - d])
        for h in range(NH):
            v = user_sum(h, (x + 1) % NX if d == 0 else (x + NX - 1) % NX)
            f = VR0[d, h].astype(F32)
            lo, hi = v[:HALF], v[HALF:]
            lo, hi = (lo + f, hi) if d == 0 else (lo, hi + f)
            VS1[d, h, :HALF] = lo.astype(BF16)
            VS1[d, h, HALF:] = hi.astype(BF16)
        put(VS1.at[d], VR1.at[d], v1.at[d], xdev[d])

    pgot(5)
    pgot(6)
    for p in (0, 1):
        for d in (0, 1):
            sum_step(d, 3, p)

    for d in (0, 1):
        got(VR1.at[d], v1.at[d], xdev[1 - d])

    def user_total(h_):
        return user_sum(h_, x) + VR1[0, h_].astype(F32) + VR1[1, h_].astype(F32)

    for j in (1, 2):
        US[j - 1] = user_total(hrel[j]).astype(BF16)
        put(US.at[j - 1], UR.at[2 - j], vz.at[2 - j], hdev[j])

    pgot(7)
    for p in (0, 1):
        for d in (0, 1):
            got(RB.at[d, 3, p], ry.at[d, 3, p], ydev[1 - d])
        q = pl.ds(y * NZ + pb[p], 2)
        ZS[pl.ds(pb[p], 2)] = (
            PS[q, core] + R[q] + RB[0, 3, p].astype(F32) + RB[1, 3, p].astype(F32)
        )
        if p == 0:
            put(ZS.at[zrel[1]], ZR.at[0], rz.at[0], zdev[1])
    for k in (2, 3):
        put(ZS.at[zrel[k]], ZR.at[k - 1], rz.at[k - 1], zdev[k])

    total = user_total(zh)
    for j in (1, 2):
        got(UR.at[j - 1], vz.at[j - 1], hdev[j])
        total = total + UR[j - 1].astype(F32)
    uo[...] = 0.5 * (ue[...] + uscale * total)

    acc = ZS[zl]
    for k in (1, 2, 3):
        got(ZR.at[k - 1], rz.at[k - 1], zdev[k])
        acc = acc + ZR[k - 1]
    io[...] = 0.5 * (ie[...] + iscale * acc)

    for c in sends:
        c.wait_send()


def on_device(user_embed, item_embed, user_degree, item_degree, tile_values, tile_rows):
    vm = pl.BlockSpec(memory_space=pltpu.VMEM)
    dma = pltpu.SemaphoreType.DMA
    user_out, item_out = pl.pallas_call(
        kernel,
        out_shape=(
            jax.ShapeDtypeStruct((TILE, D), F32),
            jax.ShapeDtypeStruct((HALF, D), F32),
        ),
        in_specs=[vm, vm, vm, vm, pl.BlockSpec(memory_space=pl.ANY), pl.BlockSpec(memory_space=pltpu.SMEM)],
        out_specs=(vm, vm),
        scratch_shapes=[
            pltpu.VMEM((COLS, NC, HALF, D), BF16),
            pltpu.VMEM((ROWS + 1, TILE, D), BF16),
            pltpu.VMEM((NT, TILE, TILE), BF16),
            pltpu.VMEM((COLS, TILE, SLOTS * TILE), BF16),
            pltpu.VMEM((NT + 1, TILE, D), F32),
            pltpu.VMEM((COLS, NC, HALF, D), F32),
            pltpu.VMEM((COLS, HALF, D), F32),
            pltpu.VMEM((2, 4, 2, 2, HALF, D), BF16),
            pltpu.VMEM((2, 4, 2, 2, HALF, D), BF16),
            pltpu.VMEM((NZ, HALF, D), F32),
            pltpu.VMEM((NZ - 1, HALF, D), F32),
            pltpu.VMEM((2, NH, HALF, D), BF16),
            pltpu.VMEM((2, NH, HALF, D), BF16),
            pltpu.VMEM((2, NH, TILE, D), BF16),
            pltpu.VMEM((2, NH, TILE, D), BF16),
            pltpu.VMEM((2, TILE, D), BF16),
            pltpu.VMEM((2, TILE, D), BF16),
            pltpu.VMEM((NT, 128), jnp.int32),
            pltpu.VMEM((8, 128), jnp.int32),
            pltpu.SMEM((8, 128), jnp.int32),
            dma(()),
            dma(()),
            dma((96,)),
            dma((3,)),
            dma((2, 4, 2)),
            dma((2, 5, 2)),
            dma((2,)),
            dma((2, 3)),
            dma((2, 3)),
            dma((8,)),
            dma((2, 4, 2)),
            dma((3,)),
            dma((2,)),
            dma((2,)),
            dma((2,)),
        ],
        compiler_params=pltpu.CompilerParams(
            collective_id=0, has_side_effects=True, vmem_limit_bytes=48 << 20
        ),
    )(
        user_embed,
        item_embed[0],
        user_degree.reshape(1, TILE),
        item_degree,
        tile_values.reshape(NT, TILE, TILE),
        tile_rows,
    )
    return user_out, item_out[None]


def solution(mesh):
    return jax.shard_map(
        on_device,
        mesh=mesh,
        in_specs=(
            P(("blk", "grp"), None),
            P("grp", "blk", None),
            P(("blk", "grp")),
            P("grp", "blk"),
            P("blk", "grp", None, None),
            P("blk", "grp"),
        ),
        out_specs=(P(("blk", "grp"), None), P("grp", "blk", None)),
        check_vma=False,
    )
```

time: 706 us -> 87.9 us (0.12)
  waiting for transfers between devices: 588 us -> 0 us
  Pallas kernels: 0 us -> 80.3 us
  blocking collectives: 47.6 us -> 0 us
  other arithmetic: 24.1 us -> 0 us
  between operations: 13.8 us -> 0.64 us
  matrix products: 11.2 us -> 0 us
  local copies, waits for them, and re-layouts: 17.2 us -> 6.69 us
    reduce_scatter x2 -> x0, waiting for transfers between devices: 458 us -> none  [the longest x1 290 us: on_device(): lax.psum_scatter(partial_items, 'blk', scatter_dimension=0, tiled=True)]
    all_gather x1 -> x0, waiting for transfers between devices: 130 us -> none  [on_device(): piece = lax.all_gather(scaled_items, 'blk', axis=0, tiled=True)]
    pallas_call x0 -> x1, Pallas kernels: none -> 80.3 us  [on_device(): pl.pallas_call(kernel, out_shape=(jax.ShapeDtypeStruct((TILE, D), F32), j...]
    all_gather x1 -> x0, blocking collectives: 47.6 us -> none  [on_device(): row_vectors = lax.all_gather(scaled_users, 'grp', axis=0, tiled=True)]
    scatter-add x1 -> x0, other arithmetic: 18.5 us -> none  [on_device(): summed.at[tile_rows.reshape(-1)].add(products.reshape(-1, tile_size, width))]
    dot_general x2 -> x0, matrix products: 11.2 us -> none  [the longest x1 6.12 us: on_device(): jnp.einsum('cstj,cjd->cstd', tiles, piece.reshape(cover, tile_size, width...]
    reshape x2 -> x0, local copies, waits for them, and re-layouts: 9.11 us -> none  [the longest x1 9.01 us: on_device(): products.reshape(-1, tile_size, width)]
  transfers between devices with their start and end apart: 3 -> 0, of which waited for: 3 -> 0; matrix products, arithmetic and copies ran while one was open for 0% -> 0% of each run, Pallas kernels for 0% -> 0%
where the time goes in v1:
time: 87.9 us; the launch traced here: 87.6 us
  Pallas kernels  80.3 us (91%)
  local copies, waits for them, and re-layouts  6.69 us (8%)
    pallas_call x1, Pallas kernels, on_device(): pl.pallas_call(kernel, out_shape=(jax.ShapeDtypeStruct((TILE, D), F32), j...  80.3 us
    unnamed x13, local copies, waits for them, and re-layouts  6.69 us

profile of v1, /device:TPU:1, one launch (start us, length us, event | category | flops | bytes accessed | tf_op | source)
XLA Modules:
  0.0 87.6 jit_solution(4067722166755955334)
XLA Ops:
  0.6 0.8 copy.8.rows
  1.4 0.0 copy-start
  1.4 1.6 %copy-done = bf16[32,2,128,128]{3,2,1,0:T(8,128)(2,1)S(1)} copy-done((bf16[32,2,128,128]{3,2,1,0:T(8,128)(2,1)S(1)}, bf16[32,2,128,128]{3,2,1,0:T(8,128)(2,1)}, u32[]{:S(2)}) %copy-start) | copy-done | bytes 2097176
  3.0 0.0 copy-start.1
  3.0 0.9 %copy-done.1 = f32[128,256]{1,0:T(8,128)S(1)} copy-done((f32[128,256]{1,0:T(8,128)S(1)}, f32[128,256]{1,0:T(8,128)}, u32[]{:S(2)}) %copy-start.1) | copy-done | bytes 131096
  3.9 0.0 copy-start.2
  3.9 0.8 copy-done.2
  4.7 0.0 copy-start.3
  4.7 0.7 copy-done.3
  5.4 0.0 copy-start.4
  5.4 0.7 copy-done.4
  6.0 80.3 %shard_map.77 = (f32[128,256]{1,0:T(8,128)S(1)}, f32[64,256]{1,0:T(8,128)S(1)}) custom-call(f32[128,256]{1,0:T(8,128)S(1)} %copy-done.1, f32[64,256]{1,0:T(8,128)S(1)} %bitcast.5, s32[1,128]{1,0:T(1,128)S(1)} %bitcast.7, s32[1,64]{1,0:T(1,128)S(1)} %copy-done.4, bf16[64,128,128]{2,1,0:T(8,128)(2,1)S(1)} %bitcast.4, s32[32,2]{1,0:T(8,128)S(1)} %copy.8.rows), custom_call_target="tpu_custom_call" | custom-call | tf_op jit(solution)/shard_map/pallas_call | solution.py:333
  86.3 0.7 copy.11
  87.0 0.6 copy.12
Async XLA Ops:
  1.4 1.6 %copy-start = (bf16[32,2,128,128]{3,2,1,0:T(8,128)(2,1)S(1)}, bf16[32,2,128,128]{3,2,1,0:T(8,128)(2,1)}, u32[]{:S(2)}) copy-start(bf16[32,2,128,128]{3,2,1,0:T(8,128)(2,1)} %param.10) | copy-start | bytes 6291460
  3.0 0.9 %copy-start.1 = (f32[128,256]{1,0:T(8,128)S(1)}, f32[128,256]{1,0:T(8,128)}, u32[]{:S(2)}) copy-start(f32[128,256]{1,0:T(8,128)} %ue.1) | copy-start | bytes 393220
  3.9 0.8 copy-start.2
  4.7 0.7 copy-start.3
  5.4 0.7 copy-start.4

commit v2 on v1

v2 whole, which is shorter than its diff:
```python
import jax
import jax.numpy as jnp
from jax import lax
from jax.experimental import pallas as pl
from jax.experimental.pallas import tpu as pltpu
from jax.sharding import PartitionSpec as P

NZ, NY, NC = 4, 8, 2
NH, NX = 3, 4
TILE = 128
HALF = 64
D = 256
COLS = NZ * NY
SLOTS = 2
NT = COLS * SLOTS
ROWS = NH * NX
F32, BF16 = jnp.float32, jnp.bfloat16
MESH = pl.DeviceIdType.MESH
GROUPS = (4, 3, -3, 2, -2, 1, -1, 0)


def valid_gather(d, s, p):
    return s <= 2 or (s == 3 and p == d)


def column(row):
    n = row.shape[1]
    a = lax.broadcasted_iota(jnp.int32, (n, n), 0)
    b = lax.broadcasted_iota(jnp.int32, (n, n), 1)
    return jnp.sum(jnp.where(a == b, jnp.broadcast_to(row, (n, n)), 0.0), axis=1, keepdims=True)


def kernel(
    ue_h, ie_h, ud_h, ideg_h, tv, rows_h, uo, io,
    X, U, T, TT, Q, S, PS, R, SB, RB, ZS, ZR, VS, VR, US, UR, keys, plan, ue, ie, ud, ideg, order, rows,
    isem, osem, send, xz, xy, xs, uz, ux, ps, ry, rz, v0, vz,
):
    b = lax.axis_index("blk")
    g = lax.axis_index("grp")
    core = b % 2
    y = (b // 2) % NY
    zl = b // (2 * NY)
    x = g % NX
    zh = g // NX
    other = 1 - core

    def blk(z_, y_, c_):
        return {"blk": (z_ * NY + y_) * NC + c_}

    def grp(h_, x_):
        return {"grp": h_ * NX + x_}

    sib = blk(zl, y, other)
    ydev = (blk(zl, (y + 1) % NY, core), blk(zl, (y + NY - 1) % NY, core))
    zrel = (zl, zl + 1 - 2 * (zl % 2), (zl + 2) % NZ, NZ - 1 - zl)
    zdev = tuple(blk(z_, y, core) for z_ in zrel)
    xrel = tuple((x + e) % NX for e in range(NX))
    xdev = tuple(grp(zh, x_) for x_ in xrel)
    hrel = (zh, (zh + NH - 1) % NH, (zh + 1) % NH)
    hdev = (None, grp(hrel[1], x), grp(hrel[2], x))
    pb0 = (zl // 2) * 2
    pb = (pb0, 2 - pb0)

    bar = pltpu.get_barrier_semaphore()
    peers = (sib,) + ydev + zdev[1:] + xdev[1:] + hdev[1:]
    for dev in peers:
        pl.semaphore_signal(bar, inc=1, device_id=dev, device_id_type=MESH)

    fetch = [
        pltpu.make_async_copy(a, v, isem.at[n])
        for n, (a, v) in enumerate(
            ((ideg_h, ideg), (ud_h, ud), (ie_h, ie), (ue_h, ue), (rows_h, rows), (tv, T))
        )
    ]
    for c in fetch:
        c.start()

    sends = []

    def put(src, dst, rsem, dev):
        c = pltpu.make_async_remote_copy(
            src_ref=src, dst_ref=dst, send_sem=send.at[len(sends)], recv_sem=rsem,
            device_id=dev, device_id_type=MESH,
        )
        c.start()
        sends.append(c)

    def got(dst, rsem, dev):
        pltpu.make_async_remote_copy(
            src_ref=dst, dst_ref=dst, send_sem=send.at[0], recv_sem=rsem,
            device_id=dev, device_id_type=MESH,
        ).wait_recv()

    for c in fetch[:4]:
        c.wait()
    iscale = column(lax.rsqrt(ideg[...].astype(F32)))
    uscale = column(lax.rsqrt(ud[...].astype(F32)))
    X[y * NZ + zl, core] = (ie[...] * iscale).astype(BF16)
    U[g] = (ue[...] * uscale).astype(BF16)
    U[ROWS] = jnp.zeros((TILE, D), BF16)

    pl.semaphore_wait(bar, len(peers))

    own = X.at[y * NZ + zl, core]
    for k in (1, 3, 2):
        put(own, own, xz.at[k - 1], zdev[k])
    for j in (1, 2):
        put(U.at[g], U.at[g], uz.at[2 - j], hdev[j])

    def users_x(j):
        s = U.at[hrel[j] * NX + x]
        for e in (2, 1, 3):
            put(s, s, ux.at[e - 1, j], xdev[e])

    users_x(0)

    def xreg(yy, p, c):
        return X.at[pl.ds(yy * NZ + pb[p], 2), c]

    def yfrom(d, s):
        return (y + NY - 1 - s) % NY if d == 0 else (y + 1 + s) % NY

    fetch[4].wait()
    for i in range(NT):
        keys[i : i + 1, :] = jnp.full((1, 128), rows[i % SLOTS, i // SLOTS], jnp.int32)
    sub = lax.broadcasted_iota(jnp.int32, (NT, 128), 0)
    lane = lax.broadcasted_iota(jnp.int32, (NT, 128), 1)
    late = (sub // SLOTS) % NY == (y + 4) % NY
    kc = keys[...]
    kl = jnp.where(late, kc + 16, kc)
    uc = kl * NT + sub
    ur = jnp.sum(jnp.where(sub == lane, uc, 0), axis=0, keepdims=True)
    ur = jnp.where(lax.broadcasted_iota(jnp.int32, (1, 128), 1) < NT, ur, 1 << 20)
    rank = jnp.sum(jnp.where(ur < uc, 1, 0), axis=1, keepdims=True)
    hit = rank == lane

    def total(m, v):
        return jnp.sum(jnp.where(m, v, 0), axis=0, keepdims=True)

    plan[...] = jnp.zeros((8, 128), jnp.int32)
    plan[0:1, :] = total(hit, sub)
    plan[1:2, :] = total(hit, kl)
    plan[2:3, :] = jnp.where(total(kl == lane, 1) > 0, total(kl <= lane, 1), 0)
    plan[3:4, :] = jnp.where(total(kl == lane + 16, 1) > 0, total(kl <= lane + 16, 1), 0)
    ocopy = pltpu.make_async_copy(plan, order, osem)
    ocopy.start()

    def xfirst(p):
        for d in (0, 1):
            put(xreg(y, p, core), xreg(y, p, core), xy.at[d, 0, p], ydev[d])

    def zgot(k):
        r = X.at[y * NZ + zrel[k], core]
        got(r, xz.at[k - 1], zdev[k])

    def flip(c, _):
        TT[c, :, 0:TILE] = T[2 * c].T
        TT[c, :, TILE:] = T[2 * c + 1].T
        return 0

    def flips(lo, hi):
        lax.fori_loop(lo, hi, flip, 0, unroll=2)

    def items_pass(s, p):
        for d in (0, 1):
            if not valid_gather(d, s, p):
                continue
            yy = yfrom(d, s)
            r = xreg(yy, p, core)
            got(r, xy.at[d, s, p], ydev[1 - d])
            if valid_gather(d, s + 1, p):
                put(r, r, xy.at[d, s + 1, p], ydev[d])
            put(r, r, xs.at[d, s, p], sib)

    def items_sib(s):
        for p in (0, 1):
            for d in (0, 1):
                if valid_gather(d, s, p):
                    got(xreg(yfrom(d, s), p, other), xs.at[d, s, p], sib)

    def products(yy):
        def one(z_, _):
            c = z_ * NY + yy
            lhs = T[pl.ds(2 * c, 2)].reshape(SLOTS * TILE, TILE)
            out = jnp.dot(lhs, X[yy * NZ + z_].reshape(TILE, D), preferred_element_type=F32)
            Q[pl.ds(2 * c, 2)] = out.reshape(SLOTS, TILE, D)
            return 0

        lax.fori_loop(0, NZ, one, 0, unroll=2)

    def partial(i):
        yd = (y + NY + GROUPS[i]) % NY

        def one(z_, _):
            c = z_ * NY + yd
            rhs = jnp.concatenate([U[rows[0, c]], U[rows[1, c]]], axis=0)
            out = jnp.dot(TT[c], rhs, preferred_element_type=F32)
            PS[yd * NZ + z_] = out.reshape(NC, HALF, D)
            return 0

        lax.fori_loop(0, NZ, one, 0, unroll=2)
        put(PS.at[pl.ds(yd * NZ, NZ), other], R.at[pl.ds(yd * NZ, NZ)], ps.at[i], sib)

    def pgot(i):
        yd = (y + NY + GROUPS[i]) % NY
        got(R.at[pl.ds(yd * NZ, NZ)], ps.at[i], sib)

    def sum_step(d, s, p):
        yd = (y + 4 - s) % NY if d == 0 else (y + NY - 4 + s) % NY
        q = pl.ds(yd * NZ + pb[p], 2)
        val = PS[q, core] + R[q]
        if not (s == 0 or (s == 1 and p != d)):
            got(RB.at[d, s - 1, p], ry.at[d, s - 1, p], ydev[1 - d])
            val = val + RB[d, s - 1, p].astype(F32)
        SB[d, s, p] = val.astype(BF16)
        put(SB.at[d, s, p], RB.at[d, s, p], ry.at[d, s, p], ydev[d])

    S[0] = jnp.zeros((TILE, D), F32)

    def running(lo, hi):
        def one(k, acc):
            keep = jnp.where(order[1, k] == order[1, jnp.maximum(k - 1, 0)], 1.0, 0.0)
            acc = acc * keep + Q[order[0, k]]
            S[k + 1] = acc
            return acc

        lax.fori_loop(lo, hi, one, jnp.zeros((TILE, D), F32), unroll=2)

    def user_sum(h_, x_):
        r = h_ * NX + x_
        return S[order[2, r]] + S[order[3, r]]

    zgot(1)
    xfirst(0)
    zgot(3)
    zgot(2)
    xfirst(1)
    r = X.at[pl.ds(y * NZ, NZ), core]
    put(r, r, xs.at[0, 4, 0], sib)

    fetch[5].wait()
    flips(0, 16)
    items_pass(0, 0)
    items_pass(0, 1)
    for j in (1, 2):
        got(U.at[hrel[j] * NX + x], uz.at[j - 1], hdev[j])
        users_x(j)
    flips(16, 32)
    r = X.at[pl.ds(y * NZ, NZ), other]
    got(r, xs.at[0, 4, 0], sib)
    products(y)
    items_pass(1, 0)
    items_pass(1, 1)
    items_sib(0)
    products((y + 1) % NY)
    products((y + NY - 1) % NY)
    for j in (0, 1, 2):
        for e in (1, 2, 3):
            got(U.at[hrel[j] * NX + xrel[e]], ux.at[3 - e, j], xdev[e])
    for i in (0, 1, 2):
        partial(i)
    items_pass(2, 0)
    items_pass(2, 1)
    for i in range(3, 8):
        partial(i)

    pgot(0)
    sum_step(0, 0, 0)
    sum_step(1, 0, 1)
    pgot(1)
    pgot(2)
    sum_step(0, 1, 1)
    sum_step(1, 1, 0)

    items_sib(1)
    products((y + 2) % NY)
    products((y + NY - 2) % NY)
    items_pass(3, 0)
    items_pass(3, 1)
    items_sib(2)
    products((y + 3) % NY)
    products((y + NY - 3) % NY)
    sum_step(0, 1, 0)
    sum_step(1, 1, 1)
    ocopy.wait()
    running(0, NT - 2 * NZ)
    items_sib(3)
    products((y + 4) % NY)
    running(NT - 2 * NZ, NT)

    for j in (1, 2, 0):
        for e in (2, 1, 3):
            VS[e - 1, j] = user_sum(hrel[j], xrel[e]).astype(BF16)
            put(VS.at[e - 1, j], VR.at[e - 1, j], v0.at[e - 1, j], xdev[e])

    pgot(3)
    pgot(4)
    for p in (0, 1):
        for d in (0, 1):
            sum_step(d, 2, p)

    def user_total(j):
        t = user_sum(hrel[j], x)
        for e in (1, 2, 3):
            got(VR.at[e - 1, j], v0.at[e - 1, j], xdev[NX - e])
            t = t + VR[e - 1, j].astype(F32)
        return t

    for j in (1, 2):
        US[j - 1] = user_total(j).astype(BF16)
        put(US.at[j - 1], UR.at[2 - j], vz.at[2 - j], hdev[j])

    pgot(5)
    pgot(6)
    for p in (0, 1):
        for d in (0, 1):
            sum_step(d, 3, p)

    utot = user_total(0)

    pgot(7)
    for p in (0, 1):
        for d in (0, 1):
            got(RB.at[d, 3, p], ry.at[d, 3, p], ydev[1 - d])
        q = pl.ds(y * NZ + pb[p], 2)
        ZS[pl.ds(pb[p], 2)] = (
            PS[q, core] + R[q] + RB[0, 3, p].astype(F32) + RB[1, 3, p].astype(F32)
        )
        if p == 0:
            put(ZS.at[zrel[1]], ZR.at[0], rz.at[0], zdev[1])
    for k in (2, 3):
        put(ZS.at[zrel[k]], ZR.at[k - 1], rz.at[k - 1], zdev[k])

    for j in (1, 2):
        got(UR.at[j - 1], vz.at[j - 1], hdev[j])
        utot = utot + UR[j - 1].astype(F32)
    uo[...] = 0.5 * (ue[...] + uscale * utot)

    acc = ZS[zl]
    for k in (1, 2, 3):
        got(ZR.at[k - 1], rz.at[k - 1], zdev[k])
        acc = acc + ZR[k - 1]
    io[...] = 0.5 * (ie[...] + iscale * acc)

    for c in sends:
        c.wait_send()


def on_device(user_embed, item_embed, user_degree, item_degree, tile_values, tile_rows):
    vm = pl.BlockSpec(memory_space=pltpu.VMEM)
    dma = pltpu.SemaphoreType.DMA
    user_out, item_out = pl.pallas_call(
        kernel,
        out_shape=(
            jax.ShapeDtypeStruct((TILE, D), F32),
            jax.ShapeDtypeStruct((HALF, D), F32),
        ),
        in_specs=[pl.BlockSpec(memory_space=pltpu.HBM)] * 6,
        out_specs=(vm, vm),
        scratch_shapes=[
            pltpu.VMEM((COLS, NC, HALF, D), BF16),
            pltpu.VMEM((ROWS + 1, TILE, D), BF16),
            pltpu.VMEM((NT, TILE, TILE), BF16),
            pltpu.VMEM((COLS, TILE, SLOTS * TILE), BF16),
            pltpu.VMEM((NT, TILE, D), F32),
            pltpu.VMEM((NT + 1, TILE, D), F32),
            pltpu.VMEM((COLS, NC, HALF, D), F32),
            pltpu.VMEM((COLS, HALF, D), F32),
            pltpu.VMEM((2, 4, 2, 2, HALF, D), BF16),
            pltpu.VMEM((2, 4, 2, 2, HALF, D), BF16),
            pltpu.VMEM((NZ, HALF, D), F32),
            pltpu.VMEM((NZ - 1, HALF, D), F32),
            pltpu.VMEM((NX - 1, NH, TILE, D), BF16),
            pltpu.VMEM((NX - 1, NH, TILE, D), BF16),
            pltpu.VMEM((2, TILE, D), BF16),
            pltpu.VMEM((2, TILE, D), BF16),
            pltpu.VMEM((NT, 128), jnp.int32),
            pltpu.VMEM((8, 128), jnp.int32),
            pltpu.VMEM((TILE, D), F32),
            pltpu.VMEM((HALF, D), F32),
            pltpu.VMEM((1, TILE), jnp.int32),
            pltpu.VMEM((1, HALF), jnp.int32),
            pltpu.SMEM((8, 128), jnp.int32),
            pltpu.SMEM((SLOTS, COLS), jnp.int32),
            dma((6,)),
            dma(()),
            dma((96,)),
            dma((3,)),
            dma((2, 4, 2)),
            dma((2, 5, 2)),
            dma((2,)),
            dma((3, 3)),
            dma((8,)),
            dma((2, 4, 2)),
            dma((3,)),
            dma((3, 3)),
            dma((2,)),
        ],
        compiler_params=pltpu.CompilerParams(
            collective_id=0, has_side_effects=True, vmem_limit_bytes=62 << 20
        ),
    )(
        user_embed,
        item_embed[0],
        user_degree.reshape(1, TILE),
        item_degree,
        tile_values.reshape(NT, TILE, TILE),
        tile_rows.T,
    )
    return user_out, item_out[None]


def solution(mesh):
    return jax.shard_map(
        on_device,
        mesh=mesh,
        in_specs=(
            P(("blk", "grp"), None),
            P("grp", "blk", None),
            P(("blk", "grp")),
            P("grp", "blk"),
            P("blk", "grp", None, None),
            P("blk", "grp"),
        ),
        out_specs=(P(("blk", "grp"), None), P("grp", "blk", None)),
        check_vma=False,
    )
```

time: 87.9 us -> 68.3 us (0.78)
  the two profiles are of different devices: /device:TPU:1 before, /device:TPU:8 now
where the time goes in v2:
time: 68.3 us; the launch traced here: 68.1 us
  Pallas kernels  64.4 us (94%)
  local copies, waits for them, and re-layouts  3.04 us (4%)
    pallas_call x1, Pallas kernels, on_device(): pl.pallas_call(kernel, out_shape=(jax.ShapeDtypeStruct((TILE, D), F32), j...  64.4 us
    unnamed x2, local copies, waits for them, and re-layouts  3.04 us

profile of v2, /device:TPU:8, one launch (start us, length us, event | category | flops | bytes accessed | tf_op | source)
XLA Modules:
  0.0 68.1 jit_solution(17492109214225551997)
XLA Ops:
  0.6 64.4 %shard_map.77 = (f32[128,256]{1,0:T(8,128)}, f32[64,256]{1,0:T(8,128)}) custom-call(f32[128,256]{1,0:T(8,128)} %ue_h.1, f32[64,256]{1,0:T(8,128)} %bitcast.7, s32[1,128]{1,0:T(1,128)} %bitcast.9, s32[1,64]{1,0:T(1,128)} %ideg_h.1, bf16[64,128,128]{2,1,0:T(8,128)(2,1)} %bitcast.5, s32[2,32]{1,0:T(2,128)} %bitcast.8), custom_call_target="tpu_custom_call" | custom-call | tf_op jit(solution)/shard_map/pallas_call | solution.py:352
  65.1 1.6 %copy.10 = f32[128,256]{1,0:T(8,128)} copy(f32[128,256]{1,0:T(8,128)} %get-tuple-element.8) | data formatting | bytes 262144
  66.6 1.5 %copy.11 = f32[1,64,256]{2,1,0:T(8,128)} copy(f32[1,64,256]{2,1,0:T(8,128)} %bitcast.6) | data formatting | bytes 131072

commit v3 on v2

v3 whole, which is shorter than its diff:
```python
import jax
import jax.numpy as jnp
from jax import lax
from jax.experimental import pallas as pl
from jax.experimental.pallas import tpu as pltpu
from jax.sharding import PartitionSpec as P

NZ, NY, NC = 4, 8, 2
NH, NX = 3, 4
TILE = 128
HALF = 64
D = 256
COLS = NZ * NY
SLOTS = 2
NT = COLS * SLOTS
ROWS = NH * NX
F32, BF16 = jnp.float32, jnp.bfloat16
MESH = pl.DeviceIdType.MESH
GROUPS = (4, 3, -3, 2, -2, 1, -1, 0)

ORDER = (
    ("flip", 0), ("flip", 1), ("flip", 2), ("flip", 3), ("sort",), ("zf", 0), ("zf", 1),
    ("prod", 0), ("ip", 0, 0, 0), ("ip", 1, 0, 0), ("uz", 1, 0), ("uz", 2, 0), ("ip", 0, 0, 1),
    ("ip", 1, 0, 1), ("prod", -1), ("prod", 1), ("uz", 1, 1), ("uz", 2, 1), ("ip", 0, 1, 0),
    ("ip", 1, 1, 0), ("ip", 0, 1, 1), ("ip", 1, 1, 1), ("prod", -2), ("prod", 2), ("ip", 0, 2, 0),
    ("ip", 1, 2, 0), ("part", 0), ("part", 1), ("part", 2), ("part", 3), ("part", 4),
    ("ip", 0, 2, 1), ("ip", 1, 2, 1), ("part", 5), ("r4", 0), ("r4", 1), ("r3", 0, 0),
    ("r3", 0, 1), ("part", 6), ("r3", 1, 1), ("r3", 1, 0), ("part", 7), ("prod", -3),
    ("ip", 0, 3, 0), ("prod", 3), ("run", 0), ("r1", 0, 0), ("r1", 0, 1), ("r1", 1, 0),
    ("ip", 1, 3, 1), ("r1", 1, 1), ("prod", 4), ("run", 1), ("vs", 1, 0), ("vs", 1, 1),
    ("vs", 2, 0), ("r2", 0, 0), ("vs", 2, 1), ("vs", 0, 0), ("r2", 1, 1), ("vs", 0, 1),
    ("r2", 0, 1), ("r2", 1, 0), ("vz", 1, 0), ("vz", 1, 1), ("vz", 2, 0), ("vz", 2, 1), ("fin", 0),
    ("fin", 1), ("iout",), ("uout",),
)


def valid_gather(d, s, p):
    return s <= 2 or (s == 3 and p == d)


def column(row):
    n = row.shape[1]
    a = lax.broadcasted_iota(jnp.int32, (n, n), 0)
    b = lax.broadcasted_iota(jnp.int32, (n, n), 1)
    return jnp.sum(jnp.where(a == b, jnp.broadcast_to(row, (n, n)), 0.0), axis=1, keepdims=True)


def kernel(
    ue_h, ie_h, ud_h, ideg_h, tv, rows_h, uo, io,
    X, U, T, TT, Q, S, PS, R, SB, RB, ZS, ZB, ZR, VS, VR, US, UR, keys, plan, ue, ie, ud, ideg, uov, iov, order, rows,
    isem, osem, wsem, send, xz, xy, xs, uz, ux, ps, ry, rz, v0, vz,
):
    b = lax.axis_index("blk")
    g = lax.axis_index("grp")
    core = b % 2
    y = (b // 2) % NY
    zl = b // (2 * NY)
    x = g % NX
    zh = g // NX
    other = 1 - core

    def blk(z_, y_, c_):
        return {"blk": (z_ * NY + y_) * NC + c_}

    def grp(h_, x_):
        return {"grp": h_ * NX + x_}

    sib = blk(zl, y, other)
    ydev = (blk(zl, (y + 1) % NY, core), blk(zl, (y + NY - 1) % NY, core))
    y2dev = (blk(zl, (y + 2) % NY, core), blk(zl, (y + NY - 2) % NY, core))
    zrel = (zl, zl + 1 - 2 * (zl % 2), (zl + 2) % NZ, NZ - 1 - zl)
    zdev = tuple(blk(z_, y, core) for z_ in zrel)
    xrel = tuple((x + e) % NX for e in range(NX))
    xdev = tuple(grp(zh, x_) for x_ in xrel)
    hrel = (zh, (zh + NH - 1) % NH, (zh + 1) % NH)
    hdev = (None, grp(hrel[1], x), grp(hrel[2], x))
    pb0 = (zl // 2) * 2
    pb = (pb0, 2 - pb0)

    bar = pltpu.get_barrier_semaphore()
    peers = (sib,) + ydev + y2dev + zdev[1:] + xdev[1:] + hdev[1:]
    for dev in peers:
        pl.semaphore_signal(bar, inc=1, device_id=dev, device_id_type=MESH)

    fetch = [
        pltpu.make_async_copy(a, v, isem.at[n])
        for n, (a, v) in enumerate(
            ((ideg_h, ideg), (ud_h, ud), (ie_h, ie), (ue_h, ue), (rows_h, rows), (tv, T))
        )
    ]
    for c in fetch:
        c.start()

    sends = []

    def put(src, dst, rsem, dev):
        c = pltpu.make_async_remote_copy(
            src_ref=src, dst_ref=dst, send_sem=send.at[len(sends)], recv_sem=rsem,
            device_id=dev, device_id_type=MESH,
        )
        c.start()
        sends.append(c)

    def got(dst, rsem, dev):
        pltpu.make_async_remote_copy(
            src_ref=dst, dst_ref=dst, send_sem=send.at[0], recv_sem=rsem,
            device_id=dev, device_id_type=MESH,
        ).wait_recv()

    for c in fetch[:4]:
        c.wait()
    iscale = column(lax.rsqrt(ideg[...].astype(F32)))
    uscale = column(lax.rsqrt(ud[...].astype(F32)))
    X[y * NZ + zl, core] = (ie[...] * iscale).astype(BF16)
    U[g] = (ue[...] * uscale).astype(BF16)
    U[ROWS] = jnp.zeros((TILE, D), BF16)

    pl.semaphore_wait(bar, len(peers))

    own = X.at[y * NZ + zl, core]
    for k in (1, 3, 2):
        put(own, own, xz.at[k - 1], zdev[k])
    def urows(j, x_, q):
        return U.at[hrel[j] * NX + x_, pl.ds(q * HALF, HALF)]

    for q in (0, 1):
        for j in (1, 2):
            put(urows(0, x, q), urows(0, x, q), uz.at[2 - j, q], hdev[j])
    for e in (2, 1, 3):
        put(U.at[g], U.at[g], ux.at[e - 1, 0, 0], xdev[e])

    def xreg(yy, p, c):
        return X.at[pl.ds(yy * NZ + pb[p], 2), c]

    def yfrom(d, s):
        return (y + NY - 1 - s) % NY if d == 0 else (y + 1 + s) % NY

    ocopy = pltpu.make_async_copy(plan, order, osem)

    def total(m, v):
        return jnp.sum(jnp.where(m, v, 0), axis=0, keepdims=True)

    def do_sort():
        fetch[4].wait()
        for i in range(NT):
            keys[i : i + 1, :] = jnp.full((1, 128), rows[i % SLOTS, i // SLOTS], jnp.int32)
        sub = lax.broadcasted_iota(jnp.int32, (NT, 128), 0)
        lane = lax.broadcasted_iota(jnp.int32, (NT, 128), 1)
        late = (sub // SLOTS) % NY == (y + 4) % NY
        kc = keys[...]
        kl = jnp.where(late, kc + 16, kc)
        uc = kl * NT + sub
        ur = jnp.sum(jnp.where(sub == lane, uc, 0), axis=0, keepdims=True)
        ur = jnp.where(lax.broadcasted_iota(jnp.int32, (1, 128), 1) < NT, ur, 1 << 20)
        rank = jnp.sum(jnp.where(ur < uc, 1, 0), axis=1, keepdims=True)
        hit = rank == lane

        plan[...] = jnp.zeros((8, 128), jnp.int32)
        plan[0:1, :] = total(hit, sub)
        plan[1:2, :] = total(hit, kl)
        plan[2:3, :] = jnp.where(total(kl == lane, 1) > 0, total(kl <= lane, 1), 0)
        plan[3:4, :] = jnp.where(total(kl == lane + 16, 1) > 0, total(kl <= lane + 16, 1), 0)
        ocopy.start()

    def xfirst(p):
        for d in (0, 1):
            put(xreg(y, p, core), xreg(y, p, core), xy.at[d, 0, p], ydev[d])

    def zgot(k):
        r = X.at[y * NZ + zrel[k], core]
        got(r, xz.at[k - 1], zdev[k])

    def flip(c, _):
        TT[c, :, 0:TILE] = T[2 * c].T
        TT[c, :, TILE:] = T[2 * c + 1].T
        return 0

    def flips(lo, hi):
        lax.fori_loop(lo, hi, flip, 0, unroll=2)

    def products(yy):
        def one(z_, _):
            c = z_ * NY + yy
            lhs = T[pl.ds(2 * c, 2)].reshape(SLOTS * TILE, TILE)
            out = jnp.dot(lhs, X[yy * NZ + z_].reshape(TILE, D), preferred_element_type=F32)
            Q[pl.ds(2 * c, 2)] = out.reshape(SLOTS, TILE, D)
            return 0

        lax.fori_loop(0, NZ, one, 0, unroll=2)

    def do_part(i):
        yd = (y + NY + GROUPS[i]) % NY
        if i == 0:
            for e in (1, 2, 3):
                got(U.at[hrel[0] * NX + xrel[e]], ux.at[3 - e, 0, 0], xdev[e])
                for j in (1, 2):
                    for q in (0, 1):
                        got(urows(j, xrel[e], q), ux.at[3 - e, j, q], xdev[e])

        def one(z_, _):
            c = z_ * NY + yd
            rhs = jnp.concatenate([U[rows[0, c]], U[rows[1, c]]], axis=0)
            out = jnp.dot(TT[c], rhs, preferred_element_type=F32)
            PS[yd * NZ + z_] = out.reshape(NC, HALF, D)
            return 0

        lax.fori_loop(0, NZ, one, 0, unroll=2)
        put(PS.at[pl.ds(yd * NZ, NZ), other], R.at[pl.ds(yd * NZ, NZ)], ps.at[i], sib)

    have = set()

    def both(n, d, p):
        i = GROUPS.index(n if d == 0 or n == 4 else -n)
        yd = (y + NY + GROUPS[i]) % NY
        if i not in have:
            have.add(i)
            got(R.at[pl.ds(yd * NZ, NZ)], ps.at[i], sib)
        q = pl.ds(yd * NZ + pb[p], 2)
        return PS[q, core] + R[q]

    def pass_on(val, d, n, dev):
        SB[d, n] = val.astype(BF16)
        put(SB.at[d, n], RB.at[d, n], ry.at[d, n], dev)

    def came(d, n):
        got(RB.at[d, n], ry.at[d, n], ydev[1 - d])
        return RB[d, n].astype(F32)

    def do_r4(d):
        pass_on(both(4, d, d), d, 0, y2dev[d])

    def do_r3(d, p):
        pass_on(both(3, d, p), d, 1 + p, ydev[d])

    def do_r2(d, p):
        val = both(2, d, p) + came(d, 1 + p)
        if p == d:
            val = val + came(d, 0)
        pass_on(val, d, 3 + p, y2dev[d])

    def do_r1(d, p):
        pass_on(both(1, d, p), d, 5 + p, ydev[d])

    def do_fin(p):
        val = both(0, 0, p)
        for d in (0, 1):
            val = val + came(d, 3 + p) + came(d, 5 + p)
        ZS[pl.ds(pb[p], 2)] = val
        ZB[pl.ds(pb[p], 2)] = val.astype(BF16)
        for k in ((1,), (2, 3))[p]:
            put(ZB.at[zrel[k]], ZR.at[k - 1], rz.at[k - 1], zdev[k])

    S[0] = jnp.zeros((TILE, D), F32)

    def running(lo, hi):
        def one(k, acc):
            keep = jnp.where(order[1, k] == order[1, jnp.maximum(k - 1, 0)], 1.0, 0.0)
            acc = acc * keep + Q[order[0, k]]
            S[k + 1] = acc
            return acc

        lax.fori_loop(lo, hi, one, jnp.zeros((TILE, D), F32), unroll=2)

    def do_run(late):
        if late:
            running(NT - 2 * NZ, NT)
        else:
            ocopy.wait()
            running(0, NT - 2 * NZ)

    def user_sum(j, x_, q):
        r = hrel[j] * NX + x_
        w = pl.ds(q * HALF, HALF)
        return S[order[2, r], w] + S[order[3, r], w]

    def do_zf(p):
        for k in ((1,), (3, 2))[p]:
            zgot(k)
        xfirst(p)
        if p == 1:
            r = X.at[pl.ds(y * NZ, NZ), core]
            put(r, r, xs.at[0, 4, 0], sib)

    def do_flip(i):
        if i == 0:
            fetch[5].wait()
        flips(i * COLS // 4, (i + 1) * COLS // 4)

    def do_ip(d, s, p):
        r = xreg(yfrom(d, s), p, core)
        got(r, xy.at[d, s, p], ydev[1 - d])
        if valid_gather(d, s + 1, p):
            put(r, r, xy.at[d, s + 1, p], ydev[d])
        put(r, r, xs.at[d, s, p], sib)

    def do_uz(j, q):
        r = urows(j, x, q)
        got(r, uz.at[j - 1, q], hdev[j])
        for e in (2, 1, 3):
            put(r, r, ux.at[e - 1, j, q], xdev[e])

    def do_prod(off):
        if off == 0:
            r = X.at[pl.ds(y * NZ, NZ), other]
            got(r, xs.at[0, 4, 0], sib)
        else:
            s = abs(off) - 1
            for d in (0, 1):
                for p in (0, 1):
                    if off == 4 and p == d or off != 4 and d == (off > 0):
                        got(xreg(yfrom(d, s), p, other), xs.at[d, s, p], sib)
        products((y + NY + off) % NY)

    def do_vs(j, q):
        w = pl.ds(q * HALF, HALF)
        for e in (2, 1, 3):
            VS[e - 1, j, w] = user_sum(j, xrel[e], q).astype(BF16)
            put(VS.at[e - 1, j, w], VR.at[e - 1, j, w], v0.at[e - 1, j, q], xdev[e])

    def user_total(j, q):
        w = pl.ds(q * HALF, HALF)
        t = user_sum(j, x, q)
        for e in (1, 2, 3):
            got(VR.at[e - 1, j, w], v0.at[e - 1, j, q], xdev[NX - e])
            t = t + VR[e - 1, j, w].astype(F32)
        return t

    def do_vz(j, q):
        w = pl.ds(q * HALF, HALF)
        US[j - 1, w] = user_total(j, q).astype(BF16)
        put(US.at[j - 1, w], UR.at[2 - j, w], vz.at[2 - j, q], hdev[j])

    out = [pltpu.make_async_copy(uov, uo, wsem.at[0]), pltpu.make_async_copy(iov, io, wsem.at[1])]

    def do_uout():
        for q in (0, 1):
            w = slice(q * HALF, (q + 1) * HALF)
            t = user_total(0, q)
            for j in (1, 2):
                got(UR.at[j - 1, pl.ds(q * HALF, HALF)], vz.at[j - 1, q], hdev[j])
                t = t + UR[j - 1, w].astype(F32)
            uov[w] = 0.5 * (ue[w] + uscale[w] * t)
        out[0].start()

    def do_iout():
        acc = ZS[zl]
        for k in (1, 2, 3):
            got(ZR.at[k - 1], rz.at[k - 1], zdev[k])
            acc = acc + ZR[k - 1].astype(F32)
        iov[...] = 0.5 * (ie[...] + iscale * acc)
        out[1].start()

    steps = {
        "zf": do_zf, "sort": do_sort, "flip": do_flip, "ip": do_ip, "uz": do_uz, "part": do_part,
        "prod": do_prod, "run": do_run, "r4": do_r4, "r3": do_r3, "r2": do_r2, "r1": do_r1,
        "fin": do_fin, "vs": do_vs, "vz": do_vz, "uout": do_uout, "iout": do_iout,
    }
    for name, *at in ORDER:
        steps[name](*at)

    for c in out:
        c.wait()
    for c in sends:
        c.wait_send()


def hand_over(a, b, c, d, sem):
    copies = [pltpu.make_async_copy(a, c, sem.at[0]), pltpu.make_async_copy(b, d, sem.at[1])]
    for c in copies:
        c.start()
    for c in copies:
        c.wait()


def on_device(user_embed, item_embed, user_degree, item_degree, tile_values, tile_rows):
    hbm = pl.BlockSpec(memory_space=pltpu.HBM)
    dma = pltpu.SemaphoreType.DMA
    shapes = (
        jax.ShapeDtypeStruct((TILE, D), F32),
        jax.ShapeDtypeStruct((HALF, D), F32),
    )
    user_out, item_out = pl.pallas_call(
        kernel,
        out_shape=shapes,
        in_specs=[hbm] * 6,
        out_specs=(hbm, hbm),
        scratch_shapes=[
            pltpu.VMEM((COLS, NC, HALF, D), BF16),
            pltpu.VMEM((ROWS + 1, TILE, D), BF16),
            pltpu.VMEM((NT, TILE, TILE), BF16),
            pltpu.VMEM((COLS, TILE, SLOTS * TILE), BF16),
            pltpu.VMEM((NT, TILE, D), F32),
            pltpu.VMEM((NT + 1, TILE, D), F32),
            pltpu.VMEM((COLS, NC, HALF, D), F32),
            pltpu.VMEM((COLS, HALF, D), F32),
            pltpu.VMEM((2, 7, 2, HALF, D), BF16),
            pltpu.VMEM((2, 7, 2, HALF, D), BF16),
            pltpu.VMEM((NZ, HALF, D), F32),
            pltpu.VMEM((NZ, HALF, D), BF16),
            pltpu.VMEM((NZ - 1, HALF, D), BF16),
            pltpu.VMEM((NX - 1, NH, TILE, D), BF16),
            pltpu.VMEM((NX - 1, NH, TILE, D), BF16),
            pltpu.VMEM((2, TILE, D), BF16),
            pltpu.VMEM((2, TILE, D), BF16),
            pltpu.VMEM((NT, 128), jnp.int32),
            pltpu.VMEM((8, 128), jnp.int32),
            pltpu.VMEM((TILE, D), F32),
            pltpu.VMEM((HALF, D), F32),
            pltpu.VMEM((1, TILE), jnp.int32),
            pltpu.VMEM((1, HALF), jnp.int32),
            pltpu.VMEM((TILE, D), F32),
            pltpu.VMEM((HALF, D), F32),
            pltpu.SMEM((8, 128), jnp.int32),
            pltpu.SMEM((SLOTS, COLS), jnp.int32),
            dma((6,)),
            dma(()),
            dma((2,)),
            dma((104,)),
            dma((3,)),
            dma((2, 4, 2)),
            dma((2, 5, 2)),
            dma((2, 2)),
            dma((3, 3, 2)),
            dma((8,)),
            dma((2, 7)),
            dma((3,)),
            dma((3, 3, 2)),
            dma((2, 2)),
        ],
        compiler_params=pltpu.CompilerParams(
            collective_id=0, has_side_effects=True, vmem_limit_bytes=62 << 20
        ),
    )(
        user_embed,
        item_embed[0],
        user_degree.reshape(1, TILE),
        item_degree,
        tile_values.reshape(NT, TILE, TILE),
        tile_rows.T,
    )
    user_out, item_out = pl.pallas_call(
        hand_over,
        out_shape=shapes,
        in_specs=[hbm] * 2,
        out_specs=(hbm, hbm),
        scratch_shapes=[dma((2,))],
        compiler_params=pltpu.CompilerParams(vmem_limit_bytes=62 << 20),
    )(user_out, item_out)
    return user_out, item_out[None]


def solution(mesh):
    return jax.shard_map(
        on_device,
        mesh=mesh,
        in_specs=(
            P(("blk", "grp"), None),
            P("grp", "blk", None),
            P(("blk", "grp")),
            P("grp", "blk"),
            P("blk", "grp", None, None),
            P("blk", "grp"),
        ),
        out_specs=(P(("blk", "grp"), None), P("grp", "blk", None)),
        check_vma=False,
    )
```

time: 68.3 us -> 71.8 us (1.051)
  the two profiles are of different devices: /device:TPU:8 before, /device:TPU:16 now
where the time goes in v3:
time: 71.8 us; the launch traced here: 71.7 us
  Pallas kernels  71 us (99%)
    pallas_call x1, Pallas kernels, on_device(): pl.pallas_call(kernel, out_shape=shapes, in_specs=[hbm] * 6, out_specs=(h...  63.9 us
    pallas_call x1, Pallas kernels, on_device(): pl.pallas_call(hand_over, out_shape=shapes, in_specs=[hbm] * 2, out_specs...  7.08 us

profile of v3, /device:TPU:16, one launch (start us, length us, event | category | flops | bytes accessed | tf_op | source)
XLA Modules:
  0.0 71.7 jit_solution(5179754347689550769)
XLA Ops:
  0.6 63.9 %shard_map.77 = (f32[128,256]{1,0:T(8,128)}, f32[64,256]{1,0:T(8,128)}) custom-call(f32[128,256]{1,0:T(8,128)} %ue_h.1, f32[64,256]{1,0:T(8,128)} %bitcast.6, s32[1,128]{1,0:T(1,128)} %bitcast.8, s32[1,64]{1,0:T(1,128)} %ideg_h.1, bf16[64,128,128]{2,1,0:T(8,128)(2,1)} %bitcast.5, s32[2,32]{1,0:T(2,128)} %bitcast.7), custom_call_target="tpu_custom_call" | custom-call | tf_op jit(solution)/shard_map/pallas_call | solution.py:382
  64.6 7.1 %shard_map.78 = (f32[128,256]{1,0:T(8,128)}, f32[64,256]{1,0:T(8,128)}) custom-call(f32[128,256]{1,0:T(8,128)} %get-tuple-element.6.a, f32[64,256]{1,0:T(8,128)} %get-tuple-element.7.b), custom_call_target="tpu_custom_call" | custom-call | tf_op jit(solution)/shard_map/pallas_call | solution.py:441

commit v4 on v3

--- a/solution.py
+++ b/solution.py
@@ -32,6 +32,7 @@
     ("r2", 0, 1), ("r2", 1, 0), ("vz", 1, 0), ("vz", 1, 1), ("vz", 2, 0), ("vz", 2, 1), ("fin", 0),
     ("fin", 1), ("iout",), ("uout",),
 )
+QU, QV = 2, 2
 
 
 def valid_gather(d, s, p):
@@ -77,6 +78,7 @@
     pb0 = (zl // 2) * 2
     pb = (pb0, 2 - pb0)
 
+    PART = TILE // QV
     bar = pltpu.get_barrier_semaphore()
     peers = (sib,) + ydev + y2dev + zdev[1:] + xdev[1:] + hdev[1:]
     for dev in peers:
@@ -121,9 +123,9 @@
     for k in (1, 3, 2):
         put(own, own, xz.at[k - 1], zdev[k])
     def urows(j, x_, q):
-        return U.at[hrel[j] * NX + x_, pl.ds(q * HALF, HALF)]
-
-    for q in (0, 1):
+        return U.at[hrel[j] * NX + x_, pl.ds(q * (TILE // QU), TILE // QU)]
+
+    for q in range(QU):
         for j in (1, 2):
             put(urows(0, x, q), urows(0, x, q), uz.at[2 - j, q], hdev[j])
     for e in (2, 1, 3):
@@ -194,7 +196,7 @@
             for e in (1, 2, 3):
                 got(U.at[hrel[0] * NX + xrel[e]], ux.at[3 - e, 0, 0], xdev[e])
                 for j in (1, 2):
-                    for q in (0, 1):
+                    for q in range(QU):
                         got(urows(j, xrel[e], q), ux.at[3 - e, j, q], xdev[e])
 
         def one(z_, _):
@@ -270,7 +272,7 @@
 
     def user_sum(j, x_, q):
         r = hrel[j] * NX + x_
-        w = pl.ds(q * HALF, HALF)
+        w = pl.ds(q * PART, PART)
         return S[order[2, r], w] + S[order[3, r], w]
 
     def do_zf(p):
@@ -312,13 +314,13 @@
         products((y + NY + off) % NY)
 
     def do_vs(j, q):
-        w = pl.ds(q * HALF, HALF)
+        w = pl.ds(q * PART, PART)
         for e in (2, 1, 3):
             VS[e - 1, j, w] = user_sum(j, xrel[e], q).astype(BF16)
             put(VS.at[e - 1, j, w], VR.at[e - 1, j, w], v0.at[e - 1, j, q], xdev[e])
 
     def user_total(j, q):
-        w = pl.ds(q * HALF, HALF)
+        w = pl.ds(q * PART, PART)
         t = user_sum(j, x, q)
         for e in (1, 2, 3):
             got(VR.at[e - 1, j, w], v0.at[e - 1, j, q], xdev[NX - e])
@@ -326,18 +328,18 @@
         return t
 
     def do_vz(j, q):
-        w = pl.ds(q * HALF, HALF)
+        w = pl.ds(q * PART, PART)
         US[j - 1, w] = user_total(j, q).astype(BF16)
         put(US.at[j - 1, w], UR.at[2 - j, w], vz.at[2 - j, q], hdev[j])
 
     out = [pltpu.make_async_copy(uov, uo, wsem.at[0]), pltpu.make_async_copy(iov, io, wsem.at[1])]
 
     def do_uout():
-        for q in (0, 1):
-            w = slice(q * HALF, (q + 1) * HALF)
+        for q in range(QV):
+            w = slice(q * PART, (q + 1) * PART)
             t = user_total(0, q)
             for j in (1, 2):
-                got(UR.at[j - 1, pl.ds(q * HALF, HALF)], vz.at[j - 1, q], hdev[j])
+                got(UR.at[j - 1, pl.ds(q * PART, PART)], vz.at[j - 1, q], hdev[j])
                 t = t + UR[j - 1, w].astype(F32)
             uov[w] = 0.5 * (ue[w] + uscale[w] * t)
         out[0].start()
@@ -364,12 +366,19 @@
         c.wait_send()
 
 
-def hand_over(a, b, c, d, sem):
-    copies = [pltpu.make_async_copy(a, c, sem.at[0]), pltpu.make_async_copy(b, d, sem.at[1])]
-    for c in copies:
-        c.start()
-    for c in copies:
-        c.wait()
+def hand_over(a, b, c, d, va, vb, sem):
+    in_a = pltpu.make_async_copy(a, va, sem.at[0])
+    in_b = pltpu.make_async_copy(b, vb, sem.at[1])
+    out_a = pltpu.make_async_copy(va, c, sem.at[2])
+    out_b = pltpu.make_async_copy(vb, d, sem.at[3])
+    in_a.start()
+    in_b.start()
+    in_a.wait()
+    out_a.start()
+    in_b.wait()
+    out_b.start()
+    out_a.wait()
+    out_b.wait()
 
 
 def on_device(user_embed, item_embed, user_degree, item_degree, tile_values, tile_rows):
@@ -443,7 +452,7 @@
         out_shape=shapes,
         in_specs=[hbm] * 2,
         out_specs=(hbm, hbm),
-        scratch_shapes=[dma((2,))],
+        scratch_shapes=[pltpu.VMEM((TILE, D), F32), pltpu.VMEM((HALF, D), F32), dma((4,))],
         compiler_params=pltpu.CompilerParams(vmem_limit_bytes=62 << 20),
     )(user_out, item_out)
     return user_out, item_out[None]

time: 71.8 us -> 66.4 us (0.925)
  Pallas kernels: 71 us -> 65.6 us
    pallas_call x1, Pallas kernels: 7.08 us -> 1.61 us  [on_device(): pl.pallas_call(hand_over, out_shape=shapes, in_specs=[hbm] * 2, out_specs...]
where the time goes in v4:
time: 66.4 us; the launch traced here: 66.2 us
  Pallas kernels  65.6 us (99%)
    pallas_call x1, Pallas kernels, on_device(): pl.pallas_call(kernel, out_shape=shapes, in_specs=[hbm] * 6, out_specs=(h...  63.9 us
    pallas_call x1, Pallas kernels, on_device(): pl.pallas_call(hand_over, out_shape=shapes, in_specs=[hbm] * 2, out_specs...  1.61 us

profile of v4, /device:TPU:16, one launch (start us, length us, event | category | flops | bytes accessed | tf_op | source)
XLA Modules:
  0.0 66.2 jit_solution(1661417942718576215)
XLA Ops:
  0.6 63.9 %shard_map.77 = (f32[128,256]{1,0:T(8,128)}, f32[64,256]{1,0:T(8,128)}) custom-call(f32[128,256]{1,0:T(8,128)} %ue_h.1, f32[64,256]{1,0:T(8,128)} %bitcast.6, s32[1,128]{1,0:T(1,128)} %bitcast.8, s32[1,64]{1,0:T(1,128)} %ideg_h.1, bf16[64,128,128]{2,1,0:T(8,128)(2,1)} %bitcast.5, s32[2,32]{1,0:T(2,128)} %bitcast.7), custom_call_target="tpu_custom_call" | custom-call | tf_op jit(solution)/shard_map/pallas_call | solution.py:391
  64.6 1.6 %shard_map.78 = (f32[128,256]{1,0:T(8,128)}, f32[64,256]{1,0:T(8,128)}) custom-call(f32[128,256]{1,0:T(8,128)} %get-tuple-element.6.a, f32[64,256]{1,0:T(8,128)} %get-tuple-element.7.b), custom_call_target="tpu_custom_call" | custom-call | tf_op jit(solution)/shard_map/pallas_call | solution.py:450

commit v5 on v4

--- a/solution.py
+++ b/solution.py
@@ -23,14 +23,14 @@
     ("prod", 0), ("ip", 0, 0, 0), ("ip", 1, 0, 0), ("uz", 1, 0), ("uz", 2, 0), ("ip", 0, 0, 1),
     ("ip", 1, 0, 1), ("prod", -1), ("prod", 1), ("uz", 1, 1), ("uz", 2, 1), ("ip", 0, 1, 0),
     ("ip", 1, 1, 0), ("ip", 0, 1, 1), ("ip", 1, 1, 1), ("prod", -2), ("prod", 2), ("ip", 0, 2, 0),
-    ("ip", 1, 2, 0), ("part", 0), ("part", 1), ("part", 2), ("part", 3), ("part", 4),
-    ("ip", 0, 2, 1), ("ip", 1, 2, 1), ("part", 5), ("r4", 0), ("r4", 1), ("r3", 0, 0),
-    ("r3", 0, 1), ("part", 6), ("r3", 1, 1), ("r3", 1, 0), ("part", 7), ("prod", -3),
-    ("ip", 0, 3, 0), ("prod", 3), ("run", 0), ("r1", 0, 0), ("r1", 0, 1), ("r1", 1, 0),
-    ("ip", 1, 3, 1), ("r1", 1, 1), ("prod", 4), ("run", 1), ("vs", 1, 0), ("vs", 1, 1),
-    ("vs", 2, 0), ("r2", 0, 0), ("vs", 2, 1), ("vs", 0, 0), ("r2", 1, 1), ("vs", 0, 1),
-    ("r2", 0, 1), ("r2", 1, 0), ("vz", 1, 0), ("vz", 1, 1), ("vz", 2, 0), ("vz", 2, 1), ("fin", 0),
-    ("fin", 1), ("iout",), ("uout",),
+    ("ip", 1, 2, 0), ("ip", 0, 2, 1), ("ip", 1, 2, 1), ("part", 0), ("part", 1), ("part", 2),
+    ("part", 3), ("part", 4), ("part", 5), ("r4", 0), ("r4", 1), ("r3", 0, 0), ("r3", 0, 1),
+    ("part", 6), ("r3", 1, 1), ("r3", 1, 0), ("part", 7), ("prod", -3), ("prod", 3),
+    ("ip", 0, 3, 0), ("ip", 1, 3, 1), ("run", 0), ("r1", 0, 0), ("r1", 0, 1), ("r1", 1, 0),
+    ("r1", 1, 1), ("prod", 4), ("run", 1), ("vs", 1, 0), ("vs", 1, 1), ("vs", 2, 0), ("r2", 0, 0),
+    ("vs", 2, 1), ("vs", 0, 0), ("r2", 1, 1), ("vs", 0, 1), ("r2", 0, 1), ("r2", 1, 0),
+    ("vz", 1, 0), ("vz", 1, 1), ("vz", 2, 0), ("vz", 2, 1), ("fin", 0), ("fin", 1), ("iout",),
+    ("uout",),
 )
 QU, QV = 2, 2
 
@@ -188,7 +188,7 @@
             Q[pl.ds(2 * c, 2)] = out.reshape(SLOTS, TILE, D)
             return 0
 
-        lax.fori_loop(0, NZ, one, 0, unroll=2)
+        lax.fori_loop(0, NZ, one, 0, unroll=4)
 
     def do_part(i):
         yd = (y + NY + GROUPS[i]) % NY
@@ -206,7 +206,7 @@
             PS[yd * NZ + z_] = out.reshape(NC, HALF, D)
             return 0
 
-        lax.fori_loop(0, NZ, one, 0, unroll=2)
+        lax.fori_loop(0, NZ, one, 0, unroll=4)
         put(PS.at[pl.ds(yd * NZ, NZ), other], R.at[pl.ds(yd * NZ, NZ)], ps.at[i], sib)
 
     have = set()

time: 66.4 us -> 65 us (0.979)
  the two profiles are of different devices: /device:TPU:16 before, /device:TPU:1 now
where the time goes in v5:
time: 65 us; the launch traced here: 63.8 us
  Pallas kernels  63.2 us (97%)
    pallas_call x1, Pallas kernels, on_device(): pl.pallas_call(kernel, out_shape=shapes, in_specs=[hbm] * 6, out_specs=(h...  61.6 us
    pallas_call x1, Pallas kernels, on_device(): pl.pallas_call(hand_over, out_shape=shapes, in_specs=[hbm] * 2, out_specs...  1.61 us

profile of v5, /device:TPU:1, one launch (start us, length us, event | category | flops | bytes accessed | tf_op | source)
XLA Modules:
  0.0 63.8 jit_solution(8164820823053829122)
XLA Ops:
  0.6 61.6 %shard_map.77 = (f32[128,256]{1,0:T(8,128)}, f32[64,256]{1,0:T(8,128)}) custom-call(f32[128,256]{1,0:T(8,128)} %ue_h.1, f32[64,256]{1,0:T(8,128)} %bitcast.6, s32[1,128]{1,0:T(1,128)} %bitcast.8, s32[1,64]{1,0:T(1,128)} %ideg_h.1, bf16[64,128,128]{2,1,0:T(8,128)(2,1)} %bitcast.5, s32[2,32]{1,0:T(2,128)} %bitcast.7), custom_call_target="tpu_custom_call" | custom-call | tf_op jit(solution)/shard_map/pallas_call | solution.py:391
  62.2 1.6 %shard_map.78 = (f32[128,256]{1,0:T(8,128)}, f32[64,256]{1,0:T(8,128)}) custom-call(f32[128,256]{1,0:T(8,128)} %get-tuple-element.6.a, f32[64,256]{1,0:T(8,128)} %get-tuple-element.7.b), custom_call_target="tpu_custom_call" | custom-call | tf_op jit(solution)/shard_map/pallas_call | solution.py:450
